TPU v7x, 512 devices: a whole 4x4x16 slice. The times are simulated.
512 devices in a mesh: group: 8 (over z_lo), member: 64 (over x, y, z_hi, core).
Axes of the slice: x: 4, y: 4, z: 16 (z_hi: 2, z_lo: 8; z = z_hi * 8 + z_lo), core: 2. Of those that a mesh axis runs over, the one named last changes fastest.
Arguments:
- embeddings: bfloat16 [262144, 1024], P(('group', 'member')), may hold values from -6 to 6
- assign: int32 [262144], P(('group', 'member')), may hold values from 0 to 255, as said below
- cluster_list: int32 [512, 64], P(('group', 'member')), may hold values from 0 to 255, as said below
- owner_map: int32 [8, 256], P('group'), may hold values from 0 to 255, as said below
- old_centroids: float32 [2048, 1024], P(('group', 'member')), may hold values from -16 to 16
Outputs:
- centroids: bfloat16 [2048, 1024], P(('group', 'member'))
- block_max: float32 [262144, 512], P(('group', 'member'))
Inputs may be any that keep to these rules, and one draw needn't show every extreme that they name: Each row of owner_map is a permutation; the centroid at position p of group g is row g * 256 + p of old_centroids and centroids. `cluster_list`: each device lists 64 distinct clusters of its group's slab. Of the 4 clusters whose positions p share p // 4, a device lists at most 2, and every device lists exactly 2 of some such set. `assign`: A cluster number within the slab of the row's group.
All inputs are finite; a program needn't handle non-finite values.
Results may differ from a plain program's by a relative error of at most 0.0023.
Values may be sent and summed in bfloat16 or wider, within the bound.
A program may use at most 64 MiB of HBM per device.

v0:
```python
import math
import jax
import jax.numpy as jnp
from jax import lax
from jax.sharding import PartitionSpec as P


def shards(embeddings, assign, cluster_list, owner_map, old_centroids):
    per_owner = old_centroids.shape[0]
    slab_rows = owner_map.shape[1]
    width = embeddings.shape[1]
    listed_ids = cluster_list[0]
    owner_row = owner_map[0]
    lookup = listed_ids[:, None] == jnp.arange(slab_rows, dtype=jnp.int32)[None, :]
    listed_pos = jnp.sum(jnp.where(lookup, owner_row[None, :], 0), axis=1)
    matched = assign[:, None] == listed_ids[None, :]
    row_target = jnp.sum(jnp.where(matched, listed_pos[None, :] + 1, 0), axis=1) - 1
    one_hot = (row_target[None, :] == jnp.arange(slab_rows, dtype=jnp.int32)[:, None]).astype(
        jnp.bfloat16
    )
    partial_value = jnp.dot(one_hot, embeddings, preferred_element_type=jnp.float32)
    tallies = jnp.sum(one_hot.astype(jnp.float32), axis=1)
    cluster_sums, counts = (
        lax.psum_scatter(partial_value, "member", scatter_dimension=0, tiled=True),
        lax.psum_scatter(tallies, "member", scatter_dimension=0, tiled=True),
    )
    updated = (cluster_sums + old_centroids) / (counts + 1.0)[:, None]
    centroids = (
        updated * lax.rsqrt(jnp.mean(updated * updated, axis=1, keepdims=True) + 1e-05)
    ).astype(jnp.bfloat16)
    inverse_root = 1.0 / math.sqrt(width)
    whole_slab = lax.all_gather(centroids, "member", axis=0, tiled=True)
    shard_rows = lax.all_gather(whole_slab, "group", axis=0, tiled=True)
    similarity = (
        lax.dot_general(
            embeddings, shard_rows, (((1,), (1,)), ((), ())), preferred_element_type=jnp.float32
        )
        * inverse_root
    )
    blocks = jnp.max(
        similarity.reshape(similarity.shape[0], shard_rows.shape[0] // per_owner, per_owner), axis=2
    )
    return (centroids, blocks)


def solution(mesh):
    in_specs = (
        P(("group", "member"), None),
        P(("group", "member")),
        P(("group", "member"), None),
        P("group", None),
        P(("group", "member"), None),
    )
    out_specs = (P(("group", "member"), None), P(("group", "member"), None))
    return jax.shard_map(shards, mesh=mesh, in_specs=in_specs, out_specs=out_specs, check_vma=False)
```

profile of v0, /device:TPU:1, one launch (start us, length us, event | category | flops | bytes accessed | tf_op | source)
XLA Modules:
  0.0 1374.8 jit_solution(14540987311990371259)
XLA Ops:
  7.2 0.0 copy-start
  7.2 0.0 all-reduce.4.cloned.1.call-start
  7.2 0.9 select_reduce_fusion.1
  8.2 0.8 select_reduce_fusion
  9.0 0.0 copy-done
  9.0 1.4 fusion.1
  10.4 0.0 all-reduce.4.cloned.1.call-update
  10.4 0.0 all-gather.3.cloned.1.call-start
  10.5 1.3 dynamic-slice
  12.4 0.1 convert_reduce_fusion
  12.5 284.2 %all-reduce.1 = f32[256]{0:T(256)S(1)} all-reduce(f32[256]{0:T(256)S(1)} %convert_reduce_fusion), channel_id=3, replica_groups=mesh['group'=8,'member'=64] {'member'}, use_global_device_ids=true, to_apply=%region_4.5.clone | all-reduce | flops 256 | bytes 2048
  296.7 0.1 dynamic-slice_add_fusion.1
  296.8 797.9 %all-reduce.4.cloned.1.call-done = f32[256,1024]{1,0:T(8,128)} async-done(((f32[256,1024]{1,0:T(8,128)}), f32[256,1024]{1,0:T(8,128)}) %all-reduce.4.cloned.1.call-update) | async-done | bytes 1048592
  1094.7 1.0 multiply_reduce_fusion
  1095.6 0.1 fusion.8
  1095.7 161.9 %all-gather = bf16[64,4,1024]{2,1,0:T(4,128)(2,1)S(1)} all-gather(bf16[1,4,1024]{2,1,0:T(4,128)(2,1)S(1)} %fusion.8), channel_id=1, replica_groups=mesh['group'=8,'member'=64] {'member'}, dimensions={0}, use_global_device_ids=true | all-gather | bytes 532480 | tf_op jit(solution)/shard_map/all_gather | solution.py:32
  1257.6 0.9 reshape.27
  1258.6 0.0 all-gather.3.cloned.1.call-update
  1258.6 0.7 multiply_convert_fusion
  1259.3 91.1 %all-gather.3.cloned.1.call-done = bf16[2048,1024]{1,0:T(8,128)(2,1)} async-done(((bf16[256,1024]{1,0:T(8,128)(2,1)}), bf16[2048,1024]{1,0:T(8,128)(2,1)}) %all-gather.3.cloned.1.call-update) | async-done | bytes 4194320 | tf_op jit(solution)/shard_map/all_gather | solution.py:33
  1350.3 6.5 multiply_bitcast_fusion
  1356.8 5.2 reshape.25
  1362.0 4.7 reduce_max.9
  1366.7 1.3 copy.8
  (3 shorter events, 0.0 us)
Async XLA Ops:
  7.2 1.8 copy-start
  7.2 1087.5 %all-reduce.4.cloned.1.call-start = ((), (), s32[]{:S(2)}) async-start(), calls=%async_computation.1 | async-start | bytes 2097152
  10.4 1339.9 %all-gather.3.cloned.1.call-start = ((), (), s32[]{:S(2)}) async-start(), calls=%async_computation | async-start | bytes 4718592 | tf_op jit(solution)/shard_map/all_gather | solution.py:33
Sparse Core Ops, SparseCore 0:
  11.5 1083.1 all-reduce.3
  1258.7 91.5 all-gather.2
where the time goes:
time: 1380 us; the launch traced here: 1370 us
  waiting for transfers between devices  889 us (64%)
  blocking collectives  446 us (32%)
  between operations  14.7 us (1%)
    unnamed x3, waiting for transfers between devices  798 us
    unnamed x1, blocking collectives  284 us
    all_gather x1, blocking collectives, shards(): whole_slab = lax.all_gather(centroids, 'member', axis=0, tiled=True)  162 us
    all_gather x1, waiting for transfers between devices, shards(): shard_rows = lax.all_gather(whole_slab, 'group', axis=0, tiled=True)  91.1 us
  transfers between devices with their start and end apart: 2, of which 2 were waited for; matrix products, arithmetic and copies ran while one was open for 0% of the time, Pallas kernels for 0%

commit v1 on v0

--- a/solution.py
+++ b/solution.py
@@ -3,6 +3,7 @@
 import jax.numpy as jnp
 from jax import lax
 from jax.sharding import PartitionSpec as P
+from jax.lax import all_to_all, axis_size
 
 
 def shards(embeddings, assign, cluster_list, owner_map, old_centroids):
@@ -29,7 +30,11 @@
         updated * lax.rsqrt(jnp.mean(updated * updated, axis=1, keepdims=True) + 1e-05)
     ).astype(jnp.bfloat16)
     inverse_root = 1.0 / math.sqrt(width)
-    whole_slab = lax.all_gather(centroids, "member", axis=0, tiled=True)
+    match_shapes = lambda inputs, along_axis: jnp.concatenate(
+        all_to_all(jnp.stack([inputs for _ in range(axis_size(along_axis))]), along_axis, 0, 0),
+        axis=0,
+    )
+    whole_slab = match_shapes(centroids, "member")
     shard_rows = lax.all_gather(whole_slab, "group", axis=0, tiled=True)
     similarity = (
         lax.dot_general(

time: 1380 us -> 1270 us (0.920)
  blocking collectives: 446 us -> 330 us
    all_gather x1 -> x0, blocking collectives: 162 us -> none  [shards(): whole_slab = lax.all_gather(centroids, 'member', axis=0, tiled=True)]
    all_to_all x0 -> x1, blocking collectives: none -> 45.6 us  [shards(): all_to_all(jnp.stack([inputs for _ in range(axis_size(along_axis))]), alo...]
where the time goes in v1:
time: 1270 us
  waiting for transfers between devices  898 us (71%)
  blocking collectives  330 us (26%)
  between operations  14.7 us (1%)
    unnamed x3, waiting for transfers between devices  798 us
    unnamed x1, blocking collectives  284 us
    all_gather x1, waiting for transfers between devices, shards(): shard_rows = lax.all_gather(whole_slab, 'group', axis=0, tiled=True)  101 us
    all_to_all x1, blocking collectives, shards(): all_to_all(jnp.stack([inputs for _ in range(axis_size(along_axis))]), alo...  45.6 us
  transfers between devices with their start and end apart: 2, of which 2 were waited for; matrix products, arithmetic and copies ran while one was open for 0% of the time, Pallas kernels for 0%

profile of v1, /device:TPU:1, one launch (start us, length us, event | category | flops | bytes accessed | tf_op | source)
XLA Modules:
  0.0 1267.4 jit_solution(13326041463018158591)
XLA Ops:
  7.2 0.0 copy-start
  7.2 0.0 all-reduce.4.cloned.1.call-start
  7.2 0.9 select_reduce_fusion.1
  8.2 0.8 select_reduce_fusion
  9.0 0.0 copy-done
  9.0 1.4 fusion.1
  10.4 0.0 all-reduce.4.cloned.1.call-update
  10.4 0.0 all-gather.2.cloned.1.call-start
  10.5 1.3 dynamic-slice
  12.4 0.1 convert_reduce_fusion
  12.5 284.2 %all-reduce.1 = f32[256]{0:T(256)S(1)} all-reduce(f32[256]{0:T(256)S(1)} %convert_reduce_fusion), channel_id=3, replica_groups=mesh['group'=8,'member'=64] {'member'}, use_global_device_ids=true, to_apply=%region_4.5.clone | all-reduce | flops 256 | bytes 2048
  296.7 0.1 dynamic-slice_add_fusion.1
  296.8 797.9 %all-reduce.4.cloned.1.call-done = f32[256,1024]{1,0:T(8,128)} async-done(((f32[256,1024]{1,0:T(8,128)}), f32[256,1024]{1,0:T(8,128)}) %all-reduce.4.cloned.1.call-update) | async-done | bytes 1048592
  1094.7 1.0 multiply_reduce_fusion
  1095.6 0.1 multiply_convert_fusion
  1095.7 0.0 copy-start.1
  1095.7 0.1 stack.2
  1095.9 45.6 %all_to_all.5 = bf16[64,4,1024]{2,1,0:T(4,128)(2,1)S(1)} all-to-all(bf16[64,4,1024]{2,1,0:T(4,128)(2,1)S(1)} %stack.2), channel_id=1, replica_groups=mesh['group'=8,'member'=64] {'member'}, dimensions={0} | all-to-all | bytes 1048576 | tf_op jit(solution)/shard_map/all_to_all | solution.py:34
  1141.4 0.9 reshape.30
  1142.4 0.0 all-gather.2.cloned.1.call-update
  1142.4 100.5 %all-gather.2.cloned.1.call-done = bf16[2048,1024]{1,0:T(8,128)(2,1)} async-done(((bf16[256,1024]{1,0:T(8,128)(2,1)}), bf16[2048,1024]{1,0:T(8,128)(2,1)}) %all-gather.2.cloned.1.call-update) | async-done | bytes 4194320 | tf_op jit(solution)/shard_map/all_gather | solution.py:38
  1242.9 6.5 multiply_bitcast_fusion
  1249.4 0.0 copy-done.1
  1249.4 5.2 reshape.31
  1254.6 4.7 reduce_max.9
  1259.3 1.3 copy.8
  (3 shorter events, 0.0 us)
Async XLA Ops:
  7.2 1.8 copy-start
  7.2 1087.5 %all-reduce.4.cloned.1.call-start = ((), (), s32[]{:S(2)}) async-start(), calls=%async_computation.2 | async-start | bytes 2097152
  10.4 1232.5 %all-gather.2.cloned.1.call-start = ((), (), s32[]{:S(2)}) async-start(), calls=%async_computation.1 | async-start | bytes 4718592 | tf_op jit(solution)/shard_map/all_gather | solution.py:38
  1095.7 153.7 %copy-start.1 = (bf16[4,1024]{1,0:T(4,128)(2,1)}, bf16[4,1024]{1,0:T(4,128)(2,1)S(1)}, u32[]{:S(2)}) copy-start(bf16[4,1024]{1,0:T(4,128)(2,1)S(1)} %multiply_convert_fusion) | copy-start | bytes 24580
Sparse Core Ops, SparseCore 0:
  11.5 1083.1 all-reduce.3
  1142.5 100.3 all-gather.1
